TPU v7x, 128 devices: a whole 4x4x4 slice. The times are simulated.
128 devices in a mesh: member: 8 (over x, z_hi), space: 16 (over y, z_lo, core).
Axes of the slice: x: 4, y: 4, z: 4 (z_hi: 2, z_lo: 2; z = z_hi * 2 + z_lo), core: 2. Of those that a mesh axis runs over, the one named last changes fastest.
Arguments:
- fields: bfloat16 [8, 100, 65536], P('member', None, 'space'), may hold values from -6 to 6
- target: bfloat16 [100, 65536], P(None, 'space'), may hold values from -6 to 6
- area_weights: float32 [65536], P('space'), may hold values from 0.25 to 5.25, as said below
- hidden: bfloat16 [8, 65536, 1024], P('member', 'space'), may hold values from -6 to 6
- w_in: bfloat16 [1024, 1024], replicated, may hold values from -0.1875 to 0.1875
- w_out: bfloat16 [100, 1024], replicated, may hold values from -0.75 to 0.75
Outputs:
- loss: float32 [], replicated
- grad_hidden: bfloat16 [8, 65536, 1024], P('member', 'space')
- grad_w1: float32 [1024, 1024], P(('member', 'space'))
Inputs may be any that keep to these rules, and one draw needn't show every extreme that they name: `area_weights`: positive area weights.
All inputs are finite; a program needn't handle non-finite values.
Results may differ from a plain program's by a relative error of at most 0.0057.
Values may be sent and summed in bfloat16 or wider, within the bound.
A program may use at most 128 MiB of HBM per device.

v0:
```python
import functools
import math

import jax
import jax.numpy as jnp
from jax import lax
from jax.experimental import pallas as pl
from jax.experimental.pallas import tpu as pltpu
from jax.sharding import PartitionSpec as P

ALPHA_FAIR = 0.95
MEMBERS, SPACES = 8, 16
CHANNELS, LOCAL, HID = 100, 4096, 1024
ROOT = math.sqrt(2.0 / math.pi)
CUBIC = 0.044715
F32, BF16 = jnp.float32, jnp.bfloat16
MESH = pl.DeviceIdType.MESH

HALF = LOCAL // 2
SHARE = HALF // MEMBERS
CHUNK = 512

BLOCKS = 4
COLS = HID // BLOCKS


def gelu_slope(u):
    s = u * u
    t = jnp.tanh(u * (ROOT + (ROOT * CUBIC) * s))
    return 0.5 * (1.0 + t) + (1.0 - t * t) * (u * (0.5 * ROOT + (1.5 * ROOT * CUBIC) * s))


def sign(a, b):
    one, zero = jnp.ones((), a.dtype), jnp.zeros((), a.dtype)
    return jnp.where(a > b, one, jnp.where(a < b, -one, zero))


class Place:
    def __init__(self):
        self.member = lax.axis_index("member")
        self.space = lax.axis_index("space")
        x, z_hi = self.member // 2, self.member % 2
        y, z_lo = self.space // 4, (self.space // 2) % 2
        self.core = self.space % 2
        self.at = (x, y, z_hi * 2 + z_lo)

    def pick(self, block, stage):
        axis = (2 * block + self.core + stage - 1) % 3
        return [(2 - axis) * (1 - axis) // 2, axis * (2 - axis), axis * (axis - 1) // 2]

    def slot(self, weights, d=0):
        return (sum(w * p for w, p in zip(weights, self.at)) + d) % 4

    def step(self, weights, d):
        at = [(p + w * d) % 4 for w, p in zip(weights, self.at)]
        return self.device(at, self.core)

    def device(self, at, core):
        x, y, z = at
        return {"member": x * 2 + z // 2, "space": (y * 2 + z % 2) * 2 + core}

    def along(self, axis, d):
        return self.step([int(axis == i) for i in range(3)], d)

    def other_core(self):
        return self.device(self.at, 1 - self.core)

    def other_member(self, d):
        return {"member": (self.member + d) % MEMBERS, "space": self.space}


def forward_kernel(
    fields, target, area, hidden, w_in, w_out,
    loss_out, held, grad_out,
    win, wout, slope, du, total,
    got, truth, weight, back, dx,
    sums, half0, sum1, part1, sum2, part2, sum3, part3,
    lacc, lsum, lpart,
    local_sems, own_sems, hid_sems, field_sems, back_sems, rs_sems, loss_sems,
):
    here = Place()
    me = here.member
    count = MEMBERS
    fair = (1.0 - ALPHA_FAIR) / count
    coef = (1.0 - fair) / (count * (count - 1))

    def share(h, member):
        return pl.ds(pl.multiple_of(h * HALF + member * SHARE, SHARE), SHARE)

    def chunk(c):
        return pl.ds(pl.multiple_of(c * CHUNK, CHUNK), CHUNK)

    def load(c):
        rows = pl.ds(pl.multiple_of(c * CHUNK, CHUNK), CHUNK)
        return pltpu.make_async_copy(hidden.at[0, rows], held.at[rows], hid_sems.at[c])

    loads = [load(c) for c in range(LOCAL // CHUNK)]
    weights = [
        pltpu.make_async_copy(src, dst, local_sems.at[i])
        for i, (src, dst) in enumerate(((w_in, win), (w_out, wout)))
    ]
    def own_copies(h):
        return [
            pltpu.make_async_copy(src, dst, own_sems.at[h, i])
            for i, (src, dst) in enumerate((
                (fields.at[0, :, share(h, me)], got.at[h, me]),
                (target.at[:, share(h, me)], truth.at[h]),
                (area.at[:, share(h, me)], weight.at[h]),
            ))
        ]

    for copy in [weights[0], *loads[:2], *own_copies(0), *loads[2:], weights[1], *own_copies(1)]:
        copy.start()

    barrier = pltpu.get_barrier_semaphore()
    others = [here.other_member(d) for d in range(1, MEMBERS)]
    others += [here.other_core()]
    others += [here.along(1, d) for d in range(1, 4)]
    others += [here.along(2, d) for d in (1, 3)]
    for device in others:
        pl.semaphore_signal(barrier, inc=1, device_id=device, device_id_type=MESH)

    def project(first, last):
        for c in range(first, last):
            loads[c].wait()

        def one_chunk(c, _):
            u = jnp.dot(held[chunk(c), :], win[...], preferred_element_type=F32)
            slope[chunk(c), :] = gelu_slope(u)
            return 0

        lax.fori_loop(first, last, one_chunk, 0)

    lacc[...] = jnp.zeros_like(lacc)
    weights[0].wait()
    project(0, 1)
    pl.semaphore_wait(barrier, len(others))

    def exchange(h, sems, source, landed):
        return [
            pltpu.make_async_remote_copy(
                src_ref=source((me + d) % MEMBERS),
                dst_ref=landed.at[h, me],
                send_sem=sems.at[0, h, d - 1],
                recv_sem=sems.at[1, h, d - 1],
                device_id=here.other_member(d),
                device_id_type=MESH,
            )
            for d in range(1, MEMBERS)
        ]

    def arrive(h, sems, landed):
        for d in range(1, MEMBERS):
            slot = landed.at[h, (me + MEMBERS - d) % MEMBERS]
            pltpu.make_async_remote_copy(
                src_ref=slot, dst_ref=slot,
                send_sem=sems.at[0, h, d - 1], recv_sem=sems.at[1, h, d - 1],
                device_id=here.other_member(MEMBERS - d), device_id_type=MESH,
            ).wait_recv()

    def field_copies(h):
        return exchange(h, field_sems, lambda to: fields.at[0, :, share(h, to)], got)

    def back_copies(h):
        return exchange(h, back_sems, lambda to: back.at[h, to], dx)

    def own_back(h):
        return pltpu.make_async_copy(back.at[h, me], dx.at[h, me], own_sems.at[h, 0])

    def compare(h, start, rows):
        at = pl.ds(start, rows)
        for j in range(0, SHARE, 128):
            lanes = pl.ds(j, 128)
            x = [got[h, k, at, lanes] for k in range(MEMBERS)]
            y = truth[h, at, lanes]
            w = weight[h, :, lanes]
            pull = coef * w
            push = w / count
            signs = [None] * MEMBERS
            for a in range(MEMBERS):
                for b in range(a + 1, MEMBERS):
                    s = sign(x[a], x[b])
                    signs[a] = s if signs[a] is None else signs[a] + s
                    signs[b] = -s if signs[b] is None else signs[b] - s
            truth_ = y.astype(F32)
            spread, miss = 0.0, 0.0
            for k in range(MEMBERS):
                own_, tally = x[k].astype(F32), signs[k].astype(F32)
                spread = spread + own_ * tally
                miss = miss + jnp.abs(own_ - truth_)
                side = sign(own_, truth_)
                back[h, k, at, lanes] = (push * side - pull * tally).astype(BF16)
            lacc[pl.ds(0, rows), :] += w * (miss / count - coef * spread)

    def compare_half(h):
        for copy in own_copies(h):
            copy.wait()
        arrive(h, field_sems, got)

        def rows16(i, _):
            compare(h, pl.multiple_of(i * 16, 16), 16)
            return 0

        whole = CHANNELS // 16
        lax.fori_loop(0, whole, rows16, 0)
        compare(h, whole * 16, CHANNELS - whole * 16)
        for copy in (own_back(h), *back_copies(h)):
            copy.start()

    def upstream(h):
        own_back(h).wait()
        arrive(h, back_sems, dx)

        for k in range(MEMBERS):
            rows = pl.ds(h * HALF + k * SHARE, SHARE)
            dv = lax.dot_general(
                dx[h, k], wout[...], (((0,), (0,)), ((), ())), preferred_element_type=F32
            )
            du[rows, :] = (dv * slope[rows, :]).astype(BF16)

    def weight_grad(h, b):
        points, cols = pl.ds(h * HALF, HALF), pl.ds(b * COLS, COLS)
        return lax.dot_general(
            held[points, :], du[points, cols], (((0,), (0,)), ((), ())), preferred_element_type=F32
        )

    def pack(b, g):
        for r in range(HID // 8):
            core = r % 2
            at = (r // 32, (r // 4) % 4, ((r // 16) % 2) * 2 + (r // 2) % 2)
            i, j, k = (at[(2 * b + core + s) % 3] for s in range(3))
            rows = g[8 * r : 8 * r + 8]
            sums[b, core, i, j, k] = jnp.concatenate([rows[:, :128], rows[:, 128:]], 0).astype(BF16)

    def rs_copies(b, stage):
        if stage == 0:
            return [pltpu.make_async_remote_copy(
                src_ref=sums.at[b, 1 - here.core], dst_ref=half0.at[b],
                send_sem=rs_sems.at[0, b, 0], recv_sem=rs_sems.at[1, b, 0],
                device_id=here.other_core(), device_id_type=MESH,
            )]
        axis = here.pick(b, stage)
        src, dst = ((sum1, part1), (sum2, part2), (sum3, part3))[stage - 1]
        copies = []
        for d in (2, 1, 3):
            k = 1 + (stage - 1) * 3 + d - 1
            copies.append(pltpu.make_async_remote_copy(
                src_ref=src.at[b, here.slot(axis, d)], dst_ref=dst.at[b, d - 1],
                send_sem=rs_sems.at[0, b, k], recv_sem=rs_sems.at[1, b, k],
                device_id=here.step(axis, d), device_id_type=MESH,
            ))
        return copies

    def rs_send(b, stage):
        for copy in rs_copies(b, stage):
            copy.start()

    def rs_sum(b, stage):
        for copy in rs_copies(b, stage):
            copy.wait_recv()
        if stage == 0:
            for p in range(4):
                sum1[b, p] = (
                    sums[b, here.core, p].astype(F32) + half0[b, p].astype(F32)
                ).astype(BF16)
            return
        src, dst = ((sum1, part1), (sum2, part2), (sum3, part3))[stage - 1]
        value = src[b, here.slot(here.pick(b, stage))].astype(F32)
        for d in range(3):
            value = value + dst[b, d].astype(F32)
        if stage == 3:
            value = value * (1.0 / math.sqrt(LOCAL * SPACES))
            grad_out[:, pl.ds(COLS * b, 128)] = value[0:8]
            grad_out[:, pl.ds(COLS * b + 128, 128)] = value[8:16]
        else:
            (sum2, sum3)[stage - 1][b] = value.astype(BF16)

    def step(b, stage):
        rs_sum(b, stage)
        if stage < 3:
            rs_send(b, stage + 1)

    def loss_copies(stage):
        copies = []
        for d in (1,) if stage == 0 else (1, 2, 3):
            k = d - 1 if stage == 0 else 1 + (stage - 1) * 3 + d - 1
            copies.append(pltpu.make_async_remote_copy(
                src_ref=lsum.at[stage],
                dst_ref=lpart.at[k],
                send_sem=loss_sems.at[0, k],
                recv_sem=loss_sems.at[1, k],
                device_id=here.other_core() if stage == 0 else here.along(stage - 1, d),
                device_id_type=MESH,
            ))
        return copies

    def loss_send(stage):
        for copy in loss_copies(stage):
            copy.start()

    def loss_step(stage):
        value = lsum[stage]
        first = 0 if stage == 0 else 1 + (stage - 1) * 3
        for d, copy in enumerate(loss_copies(stage)):
            copy.wait_recv()
            value = value + lpart[first + d]
        lsum[stage + 1] = value
        if stage < 3:
            loss_send(stage + 1)

    for copy in field_copies(0):
        copy.start()
    project(1, 3)
    for copy in field_copies(1):
        copy.start()
    project(3, 5)
    compare_half(0)
    project(5, 7)
    compare_half(1)
    project(7, 8)
    weights[1].wait()
    upstream(0)
    for b in range(BLOCKS):
        total[:, pl.ds(b * COLS, COLS)] = weight_grad(0, b)
    upstream(1)
    lsum[0] = lacc[0:8, :] + lacc[8:16, :]
    for b in range(BLOCKS):
        pack(b, total[:, pl.ds(b * COLS, COLS)] + weight_grad(1, b))
        rs_send(b, 0)
        if b == 0:
            loss_send(0)
        else:
            step(b - 1, 0)
        if b == 1:
            loss_step(0)
    between = (
        ((3, 0),),
        ((0, 1),),
        ((1, 1),),
        ((2, 1),),
        ((3, 1), (0, 2)),
        ((1, 2), (2, 2)),
        ((3, 2), (0, 3)),
        ((1, 3), (2, 3), (3, 3)),
    )

    for c, steps in enumerate(between):
        held[chunk(c), :] = lax.dot_general(
            du[chunk(c), :], win[...], (((1,), (1,)), ((), ())), preferred_element_type=F32
        ).astype(BF16)
        for b, stage in steps:
            step(b, stage)
            if b == 0:
                loss_step(stage)
    loss_out[0, 0] = jnp.sum(lsum[4]) / (CHANNELS * LOCAL * SPACES)

    for h in range(2):
        for copy in field_copies(h) + back_copies(h):
            copy.wait_send()
    for stage in range(4):
        for copy in loss_copies(stage):
            copy.wait_send()
        for b in range(BLOCKS):
            for copy in rs_copies(b, stage):
                copy.wait_send()


def on_device(fields, target, area_weights, hidden, w_in, w_out):
    anywhere = pl.BlockSpec(memory_space=pl.ANY)
    vmem = pl.BlockSpec(memory_space=pltpu.VMEM)
    dma = pltpu.SemaphoreType.DMA
    tile = (16, 128)
    loss, grad_hidden, grad_w1 = pl.pallas_call(
        forward_kernel,
        out_shape=(
            jax.ShapeDtypeStruct((1, 1), F32),
            pltpu.VMEM((LOCAL, HID), BF16),
            pltpu.VMEM((8, HID), F32),
        ),
        in_specs=[anywhere] * 6,
        out_specs=(pl.BlockSpec(memory_space=pltpu.SMEM), vmem, vmem),
        scratch_shapes=[
            pltpu.VMEM((HID, HID), BF16),
            pltpu.VMEM((CHANNELS, HID), BF16),
            pltpu.VMEM((LOCAL, HID), F32),
            pltpu.VMEM((LOCAL, HID), BF16),
            pltpu.VMEM((HID, HID), F32),
            pltpu.VMEM((2, MEMBERS, CHANNELS, SHARE), BF16),
            pltpu.VMEM((2, CHANNELS, SHARE), BF16),
            pltpu.VMEM((2, 1, SHARE), F32),
            pltpu.VMEM((2, MEMBERS, CHANNELS, SHARE), BF16),
            pltpu.VMEM((2, MEMBERS, CHANNELS, SHARE), BF16),
            pltpu.VMEM((BLOCKS, 2, 4, 4, 4) + tile, BF16),
            pltpu.VMEM((BLOCKS, 4, 4, 4) + tile, BF16),
            pltpu.VMEM((BLOCKS, 4, 4, 4) + tile, BF16),
            pltpu.VMEM((BLOCKS, 3, 4, 4) + tile, BF16),
            pltpu.VMEM((BLOCKS, 4, 4) + tile, BF16),
            pltpu.VMEM((BLOCKS, 3, 4) + tile, BF16),
            pltpu.VMEM((BLOCKS, 4) + tile, BF16),
            pltpu.VMEM((BLOCKS, 3) + tile, BF16),
            pltpu.VMEM((16, 128), F32),
            pltpu.VMEM((5, 8, 128), F32),
            pltpu.VMEM((10, 8, 128), F32),
            dma((2,)),
            dma((2, 3)),
            dma((LOCAL // CHUNK,)),
            dma((2, 2, MEMBERS - 1)),
            dma((2, 2, MEMBERS - 1)),
            dma((2, BLOCKS, 10)),
            dma((2, 10)),
        ],
        compiler_params=pltpu.CompilerParams(
            collective_id=0, has_side_effects=True, vmem_limit_bytes=52 * 2**20
        ),
        cost_estimate=pl.CostEstimate(
            flops=2 * LOCAL * HID * (3 * HID + CHANNELS),
            bytes_accessed=12 * 2**20,
            transcendentals=LOCAL * HID,
        ),
    )(fields, target, area_weights[None, :], hidden, w_in, w_out)
    return (loss[0, 0], grad_hidden[None], grad_w1)


def solution(mesh):
    return jax.shard_map(
        on_device,
        mesh=mesh,
        in_specs=(
            P("member", None, "space"),
            P(None, "space"),
            P("space"),
            P("member", "space", None),
            P(),
            P(),
        ),
        out_specs=(P(), P("member", "space", None), P(("member", "space"), None)),
        check_vma=False,
    )
```

profile of v0, /device:TPU:0, one launch (start us, length us, event | category | flops | bytes accessed | tf_op | source)
XLA Modules:
  0.0 69.8 jit_solution(16503541841060492743)
XLA Ops:
  0.6 63.4 %shard_map.85 = (f32[1,1]{1,0:T(1,128)}, bf16[4096,1024]{1,0:T(8,128)(2,1)S(1)}, f32[8,1024]{1,0:T(8,128)S(1)}) custom-call(bf16[1,100,4096]{2,1,0:T(8,128)(2,1)} %fields.1, bf16[100,4096]{1,0:T(8,128)(2,1)} %target.1, f32[1,4096]{1,0:T(1,128)} %bitcast.4, bf16[1,4096,1024]{2,1,0:T(8,128)(2,1)} %hidden.1, bf16[1024,1024]{1,0:T(8,128)(2,1)} %w_in.1, ...), custom_call_target="tpu_custom_call" | custom-call | flops 26608664576 | bytes 12582912 | tf_op jit(solution)/shard_map/pallas_call | solution.py:373
  64.1 3.4 %copy.12 = bf16[1,4096,1024]{2,1,0:T(8,128)(2,1)} copy(bf16[1,4096,1024]{2,1,0:T(8,128)(2,1)S(1)} %bitcast.3) | data formatting | bytes 16777216
  67.5 0.6 copy.13
where the time goes:
time: 69.9 us; the launch traced here: 69.8 us
  Pallas kernels  63.4 us (91%)
  local copies, waits for them, and re-layouts  4.01 us (6%)
  between operations  2.33 us (3%)
    pallas_call x1, Pallas kernels, on_device(): pl.pallas_call(forward_kernel, out_shape=(jax.ShapeDtypeStruct((1, 1), F3...  63.4 us
    unnamed x2, local copies, waits for them, and re-layouts  4.01 us

commit v1 on v0

--- a/solution.py
+++ b/solution.py
@@ -21,6 +21,7 @@
 CHUNK = 512
 
 BLOCKS = 4
+GROUPS = BLOCKS // 2
 COLS = HID // BLOCKS
 
 
@@ -44,8 +45,8 @@
         self.core = self.space % 2
         self.at = (x, y, z_hi * 2 + z_lo)
 
-    def pick(self, block, stage):
-        axis = (2 * block + self.core + stage - 1) % 3
+    def pick(self, place):
+        axis = (2 * self.core + place) % 3
         return [(2 - axis) * (1 - axis) // 2, axis * (2 - axis), axis * (axis - 1) // 2]
 
     def slot(self, weights, d=0):
@@ -54,6 +55,10 @@
     def step(self, weights, d):
         at = [(p + w * d) % 4 for w, p in zip(weights, self.at)]
         return self.device(at, self.core)
+
+    def in_plane(self, d, e):
+        pairs = zip(self.at, self.pick(1), self.pick(2))
+        return self.device([(p + v * d + w * e) % 4 for p, v, w in pairs], self.core)
 
     def device(self, at, core):
         x, y, z = at
@@ -74,9 +79,9 @@
     loss_out, held, grad_out,
     win, wout, slope, du, total,
     got, truth, weight, back, dx,
-    sums, half0, sum1, part1, sum2, part2, sum3, part3,
+    sums, half0, sum1, part1, sum2, part2,
     lacc, lsum, lpart,
-    local_sems, own_sems, hid_sems, field_sems, back_sems, rs_sems, loss_sems,
+    local_sems, own_sems, hid_sems, field_sems, back_sems, rs_sems, plane_sems, loss_sems,
 ):
     here = Place()
     me = here.member
@@ -117,6 +122,7 @@
     others += [here.other_core()]
     others += [here.along(1, d) for d in range(1, 4)]
     others += [here.along(2, d) for d in (1, 3)]
+    others += [here.in_plane(d, e) for d in range(1, 4) for e in range(1, 4)]
     for device in others:
         pl.semaphore_signal(barrier, inc=1, device_id=device, device_id_type=MESH)
 
@@ -132,8 +138,6 @@
         lax.fori_loop(first, last, one_chunk, 0)
 
     lacc[...] = jnp.zeros_like(lacc)
-    weights[0].wait()
-    project(0, 1)
     pl.semaphore_wait(barrier, len(others))
 
     def exchange(h, sems, source, landed):
@@ -228,7 +232,7 @@
         for r in range(HID // 8):
             core = r % 2
             at = (r // 32, (r // 4) % 4, ((r // 16) % 2) * 2 + (r // 2) % 2)
-            i, j, k = (at[(2 * b + core + s) % 3] for s in range(3))
+            i, j, k = (at[(2 * core + s) % 3] for s in range(3))
             rows = g[8 * r : 8 * r + 8]
             sums[b, core, i, j, k] = jnp.concatenate([rows[:, :128], rows[:, 128:]], 0).astype(BF16)
 
@@ -239,17 +243,15 @@
                 send_sem=rs_sems.at[0, b, 0], recv_sem=rs_sems.at[1, b, 0],
                 device_id=here.other_core(), device_id_type=MESH,
             )]
-        axis = here.pick(b, stage)
-        src, dst = ((sum1, part1), (sum2, part2), (sum3, part3))[stage - 1]
-        copies = []
-        for d in (2, 1, 3):
-            k = 1 + (stage - 1) * 3 + d - 1
-            copies.append(pltpu.make_async_remote_copy(
-                src_ref=src.at[b, here.slot(axis, d)], dst_ref=dst.at[b, d - 1],
-                send_sem=rs_sems.at[0, b, k], recv_sem=rs_sems.at[1, b, k],
+        axis = here.pick(0)
+        return [
+            pltpu.make_async_remote_copy(
+                src_ref=sum1.at[b, here.slot(axis, d)], dst_ref=part1.at[b, d - 1],
+                send_sem=rs_sems.at[0, b, d], recv_sem=rs_sems.at[1, b, d],
                 device_id=here.step(axis, d), device_id_type=MESH,
-            ))
-        return copies
+            )
+            for d in (2, 1, 3)
+        ]
 
     def rs_send(b, stage):
         for copy in rs_copies(b, stage):
@@ -264,21 +266,47 @@
                     sums[b, here.core, p].astype(F32) + half0[b, p].astype(F32)
                 ).astype(BF16)
             return
-        src, dst = ((sum1, part1), (sum2, part2), (sum3, part3))[stage - 1]
-        value = src[b, here.slot(here.pick(b, stage))].astype(F32)
+        value = sum1[b, here.slot(here.pick(0))].astype(F32)
         for d in range(3):
-            value = value + dst[b, d].astype(F32)
-        if stage == 3:
-            value = value * (1.0 / math.sqrt(LOCAL * SPACES))
-            grad_out[:, pl.ds(COLS * b, 128)] = value[0:8]
-            grad_out[:, pl.ds(COLS * b + 128, 128)] = value[8:16]
-        else:
-            (sum2, sum3)[stage - 1][b] = value.astype(BF16)
+            value = value + part1[b, d].astype(F32)
+        sum2[b // 2, :, :, b % 2] = value.astype(BF16)
+
+    def plane_copies(g):
+        v, w = here.pick(1), here.pick(2)
+        return [
+            pltpu.make_async_remote_copy(
+                src_ref=sum2.at[g, here.slot(v, d), here.slot(w, e)],
+                dst_ref=part2.at[g, d * 4 + e - 1],
+                send_sem=plane_sems.at[0, g, d * 4 + e - 1],
+                recv_sem=plane_sems.at[1, g, d * 4 + e - 1],
+                device_id=here.in_plane(d, e),
+                device_id_type=MESH,
+            )
+            for d in (2, 1, 3, 0)
+            for e in (2, 1, 3, 0)
+            if (d, e) != (0, 0)
+        ]
+
+    def plane_send(g):
+        for copy in plane_copies(g):
+            copy.start()
+
+    def plane_sum(g):
+        value = sum2[g, here.slot(here.pick(1)), here.slot(here.pick(2))].astype(F32)
+        for copy in plane_copies(g):
+            copy.wait_recv()
+        for n in range(15):
+            value = value + part2[g, n].astype(F32)
+        value = value * (1.0 / math.sqrt(LOCAL * SPACES))
+        for q in range(2):
+            at = COLS * (2 * g + q)
+            grad_out[:, pl.ds(at, 128)] = value[q, 0:8]
+            grad_out[:, pl.ds(at + 128, 128)] = value[q, 8:16]
 
     def step(b, stage):
         rs_sum(b, stage)
-        if stage < 3:
-            rs_send(b, stage + 1)
+        if stage == 0:
+            rs_send(b, 1)
 
     def loss_copies(stage):
         copies = []
@@ -310,7 +338,8 @@
 
     for copy in field_copies(0):
         copy.start()
-    project(1, 3)
+    weights[0].wait()
+    project(0, 3)
     for copy in field_copies(1):
         copy.start()
     project(3, 5)
@@ -322,36 +351,39 @@
     upstream(0)
     for b in range(BLOCKS):
         total[:, pl.ds(b * COLS, COLS)] = weight_grad(0, b)
+    lsum[0] = lacc[0:8, :] + lacc[8:16, :]
+    loss_send(0)
     upstream(1)
-    lsum[0] = lacc[0:8, :] + lacc[8:16, :]
     for b in range(BLOCKS):
         pack(b, total[:, pl.ds(b * COLS, COLS)] + weight_grad(1, b))
         rs_send(b, 0)
-        if b == 0:
-            loss_send(0)
-        else:
+        if b > 0:
             step(b - 1, 0)
-        if b == 1:
-            loss_step(0)
-    between = (
-        ((3, 0),),
-        ((0, 1),),
-        ((1, 1),),
-        ((2, 1),),
-        ((3, 1), (0, 2)),
-        ((1, 2), (2, 2)),
-        ((3, 2), (0, 3)),
-        ((1, 3), (2, 3), (3, 3)),
-    )
-
-    for c, steps in enumerate(between):
+
+    def first_plane():
+        step(0, 1)
+        step(1, 1)
+        plane_send(0)
+
+    def second_plane():
+        step(2, 1)
+        step(3, 1)
+        plane_send(1)
+
+    between = {
+        0: lambda: (step(3, 0), loss_step(0)),
+        2: lambda: (first_plane(), loss_step(1)),
+        4: lambda: (second_plane(), loss_step(2)),
+        7: lambda: plane_sum(0),
+    }
+    for c in range(LOCAL // CHUNK):
         held[chunk(c), :] = lax.dot_general(
             du[chunk(c), :], win[...], (((1,), (1,)), ((), ())), preferred_element_type=F32
         ).astype(BF16)
-        for b, stage in steps:
-            step(b, stage)
-            if b == 0:
-                loss_step(stage)
+        if c in between:
+            between[c]()
+    loss_step(3)
+    plane_sum(1)
     loss_out[0, 0] = jnp.sum(lsum[4]) / (CHANNELS * LOCAL * SPACES)
 
     for h in range(2):
@@ -360,9 +392,12 @@
     for stage in range(4):
         for copy in loss_copies(stage):
             copy.wait_send()
-        for b in range(BLOCKS):
-            for copy in rs_copies(b, stage):
-                copy.wait_send()
+    for b in range(BLOCKS):
+        for copy in rs_copies(b, 0) + rs_copies(b, 1):
+            copy.wait_send()
+    for g in range(GROUPS):
+        for copy in plane_copies(g):
+            copy.wait_send()
 
 
 def on_device(fields, target, area_weights, hidden, w_in, w_out):
@@ -394,10 +429,8 @@
             pltpu.VMEM((BLOCKS, 4, 4, 4) + tile, BF16),
             pltpu.VMEM((BLOCKS, 4, 4, 4) + tile, BF16),
             pltpu.VMEM((BLOCKS, 3, 4, 4) + tile, BF16),
-            pltpu.VMEM((BLOCKS, 4, 4) + tile, BF16),
-            pltpu.VMEM((BLOCKS, 3, 4) + tile, BF16),
-            pltpu.VMEM((BLOCKS, 4) + tile, BF16),
-            pltpu.VMEM((BLOCKS, 3) + tile, BF16),
+            pltpu.VMEM((GROUPS, 4, 4, 2) + tile, BF16),
+            pltpu.VMEM((GROUPS, 15, 2) + tile, BF16),
             pltpu.VMEM((16, 128), F32),
             pltpu.VMEM((5, 8, 128), F32),
             pltpu.VMEM((10, 8, 128), F32),
@@ -406,7 +439,8 @@
             dma((LOCAL // CHUNK,)),
             dma((2, 2, MEMBERS - 1)),
             dma((2, 2, MEMBERS - 1)),
-            dma((2, BLOCKS, 10)),
+            dma((2, BLOCKS, 4)),
+            dma((2, GROUPS, 15)),
             dma((2, 10)),
         ],
         compiler_params=pltpu.CompilerParams(

time: 69.9 us -> 66.3 us (0.948)
  Pallas kernels: 63.4 us -> 59.8 us
    pallas_call x1, Pallas kernels: 63.4 us -> 59.8 us  [on_device(): pl.pallas_call(forward_kernel, out_shape=(jax.ShapeDtypeStruct((1, 1), F3...]
where the time goes in v1:
time: 66.3 us; the launch traced here: 66.1 us
  Pallas kernels  59.8 us (90%)
  local copies, waits for them, and re-layouts  4.01 us (6%)
  between operations  2.33 us (4%)
    pallas_call x1, Pallas kernels, on_device(): pl.pallas_call(forward_kernel, out_shape=(jax.ShapeDtypeStruct((1, 1), F3...  59.8 us
    unnamed x2, local copies, waits for them, and re-layouts  4.01 us

profile of v1, /device:TPU:0, one launch (start us, length us, event | category | flops | bytes accessed | tf_op | source)
XLA Modules:
  0.0 66.1 jit_solution(12386445203804086318)
XLA Ops:
  0.6 59.8 %shard_map.85 = (f32[1,1]{1,0:T(1,128)}, bf16[4096,1024]{1,0:T(8,128)(2,1)S(1)}, f32[8,1024]{1,0:T(8,128)S(1)}) custom-call(bf16[1,100,4096]{2,1,0:T(8,128)(2,1)} %fields.1, bf16[100,4096]{1,0:T(8,128)(2,1)} %target.1, f32[1,4096]{1,0:T(1,128)} %bitcast.4, bf16[1,4096,1024]{2,1,0:T(8,128)(2,1)} %hidden.1, bf16[1024,1024]{1,0:T(8,128)(2,1)} %w_in.1, ...), custom_call_target="tpu_custom_call" | custom-call | flops 26608664576 | bytes 12582912 | tf_op jit(solution)/shard_map/pallas_call | solution.py:408
  60.4 3.4 %copy.12 = bf16[1,4096,1024]{2,1,0:T(8,128)(2,1)} copy(bf16[1,4096,1024]{2,1,0:T(8,128)(2,1)S(1)} %bitcast.3) | data formatting | bytes 16777216
  63.8 0.6 copy.13

commit v2 on v1

--- a/solution.py
+++ b/solution.py
@@ -19,6 +19,7 @@
 HALF = LOCAL // 2
 SHARE = HALF // MEMBERS
 CHUNK = 512
+STORES = 4
 
 BLOCKS = 4
 GROUPS = BLOCKS // 2
@@ -130,12 +131,9 @@
         for c in range(first, last):
             loads[c].wait()
 
-        def one_chunk(c, _):
-            u = jnp.dot(held[chunk(c), :], win[...], preferred_element_type=F32)
-            slope[chunk(c), :] = gelu_slope(u)
-            return 0
-
-        lax.fori_loop(first, last, one_chunk, 0)
+        rows = pl.ds(first * CHUNK, (last - first) * CHUNK)
+        u = jnp.dot(held[rows, :], win[...], preferred_element_type=F32)
+        slope[rows, :] = gelu_slope(u)
 
     lacc[...] = jnp.zeros_like(lacc)
     pl.semaphore_wait(barrier, len(others))
@@ -339,10 +337,11 @@
     for copy in field_copies(0):
         copy.start()
     weights[0].wait()
-    project(0, 3)
+    project(0, 2)
     for copy in field_copies(1):
         copy.start()
-    project(3, 5)
+    project(2, 4)
+    project(4, 5)
     compare_half(0)
     project(5, 7)
     compare_half(1)
@@ -398,6 +397,19 @@
     for g in range(GROUPS):
         for copy in plane_copies(g):
             copy.wait_send()
+
+
+def store_kernel(grad_hidden, grad_w1, hidden_out, w1_out, sems):
+    copies = [pltpu.make_async_copy(grad_w1, w1_out, sems.at[STORES])]
+    for i in range(STORES):
+        rows = pl.ds(i * (LOCAL // STORES), LOCAL // STORES)
+        copies.append(
+            pltpu.make_async_copy(grad_hidden.at[rows], hidden_out.at[0, rows], sems.at[i])
+        )
+    for copy in copies:
+        copy.start()
+    for copy in copies:
+        copy.wait()
 
 
 def on_device(fields, target, area_weights, hidden, w_in, w_out):
@@ -452,7 +464,19 @@
             transcendentals=LOCAL * HID,
         ),
     )(fields, target, area_weights[None, :], hidden, w_in, w_out)
-    return (loss[0, 0], grad_hidden[None], grad_w1)
+    vmem_in = [pltpu.with_memory_space_constraint(a, pltpu.VMEM) for a in (grad_hidden, grad_w1)]
+    grad_hidden, grad_w1 = pl.pallas_call(
+        store_kernel,
+        out_shape=(
+            jax.ShapeDtypeStruct((1, LOCAL, HID), BF16),
+            jax.ShapeDtypeStruct((8, HID), F32),
+        ),
+        in_specs=[vmem, vmem],
+        out_specs=(anywhere, anywhere),
+        scratch_shapes=[dma((STORES + 1,))],
+        compiler_params=pltpu.CompilerParams(vmem_limit_bytes=2**20),
+    )(*vmem_in)
+    return (loss[0, 0], grad_hidden, grad_w1)
 
 
 def solution(mesh):

time: 66.3 us -> 65.3 us (0.985)
  local copies, waits for them, and re-layouts: 4.01 us -> 0 us
  Pallas kernels: 59.8 us -> 62.8 us
    unnamed x2 -> x0, local copies, waits for them, and re-layouts: 4.01 us -> none
    pallas_call x0 -> x1, Pallas kernels: none -> 3.39 us  [on_device(): pl.pallas_call(store_kernel, out_shape=(jax.ShapeDtypeStruct((1, LOCAL, H...]
where the time goes in v2:
time: 65.3 us; the launch traced here: 65.2 us
  Pallas kernels  62.8 us (96%)
  between operations  2.41 us (4%)
    pallas_call x1, Pallas kernels, on_device(): pl.pallas_call(forward_kernel, out_shape=(jax.ShapeDtypeStruct((1, 1), F3...  59.4 us
    pallas_call x1, Pallas kernels, on_device(): pl.pallas_call(store_kernel, out_shape=(jax.ShapeDtypeStruct((1, LOCAL, H...  3.39 us

profile of v2, /device:TPU:0, one launch (start us, length us, event | category | flops | bytes accessed | tf_op | source)
XLA Modules:
  0.0 65.2 jit_solution(12850728342732882094)
XLA Ops:
  0.6 59.4 %shard_map.85 = (f32[1,1]{1,0:T(1,128)}, bf16[4096,1024]{1,0:T(8,128)(2,1)S(1)}, f32[8,1024]{1,0:T(8,128)S(1)}) custom-call(bf16[1,100,4096]{2,1,0:T(8,128)(2,1)} %fields.1, bf16[100,4096]{1,0:T(8,128)(2,1)} %target.1, f32[1,4096]{1,0:T(1,128)} %bitcast.2, bf16[1,4096,1024]{2,1,0:T(8,128)(2,1)} %hidden.1, bf16[1024,1024]{1,0:T(8,128)(2,1)} %w_in.1, ...), custom_call_target="tpu_custom_call" | custom-call | flops 26608664576 | bytes 12582912 | tf_op jit(solution)/shard_map/pallas_call | solution.py:420
  60.0 3.4 %shard_map.86 = (bf16[1,4096,1024]{2,1,0:T(8,128)(2,1)}, f32[8,1024]{1,0:T(8,128)}) custom-call(bf16[4096,1024]{1,0:T(8,128)(2,1)S(1)} %get-tuple-element.9.grad_hidden, f32[8,1024]{1,0:T(8,128)S(1)} %get-tuple-element.10.grad_w1), custom_call_target="tpu_custom_call" | custom-call | tf_op jit(solution)/shard_map/pallas_call | solution.py:468
